TPU v7x, 32 devices: a whole 2x2x4 slice. The times are simulated.
32 devices in a mesh: prow: 8 (over z, y), pcol: 4 (over x, core).
Axes of the slice: x: 2, y: 2, z: 4, core: 2. Of those that a mesh axis runs over, the one named last changes fastest.
Arguments:
- panels: float32 [7, 32768], P(None, ('prow', 'pcol')), may hold values from -6 to 8, as said below
- slab_ids: int32 [1024], replicated, may hold values from 0 to 32767, as said below
- pivots: int32 [512], replicated, may hold values from 0 to 65535, as said below
Outputs:
- head: float32 [4, 4, 64, 2, 512], P('pcol')
- lower: float32 [4, 1, 64, 2, 2, 32768], P('pcol', None, None, None, None, 'prow')
- trailing: float32 [4, 3, 64, 2, 2, 32768], P('pcol', None, None, None, None, 'prow')
Inputs may be any that keep to these rules, and one draw needn't show every extreme that they name: x in -6 to 6, y in -1 to 1, z in -0.5 to 0 (lid panels have z = 0), area from 0.3 / 256 to 3 / 256, half size 0.02 to 0.05, both self parts 4 to 8. `slab_ids`: 1024 different panel numbers. pivots[2 k] and pivots[2 k + 1] are 2 slab_ids[k] and 2 slab_ids[k] + 1, in either order.
All inputs are finite; a program needn't handle non-finite values.
Results may differ from a plain program's by a relative error of at most 0.0003.
Values sent between devices are 32-bit elements; how exact they have to be, the bound alone decides.
A program may use at most 128 MiB of HBM per device.

v0:
```python
import jax
import jax.numpy as jnp
import numpy as np
from jax import lax
from jax.sharding import PartitionSpec as P

QUAD_OFFSET = 0.5773502691896258
WAVE_NUMBER = 6.0


def influence(row_geometry, row_panels, col_geometry, col_panels):
    target_x = row_geometry[0][None, :]
    target_y = row_geometry[1][None, :]
    target_z = row_geometry[2][None, :]
    source_x = col_geometry[0][:, None]
    source_y = col_geometry[1][:, None]
    source_z = col_geometry[2][:, None]
    areas = col_geometry[3][:, None]
    halfsize = col_geometry[4][:, None]
    halfsq = halfsize * halfsize
    below = target_z - source_z
    mirror = target_z + source_z
    depth_factor = 2.0 * WAVE_NUMBER * jnp.exp(WAVE_NUMBER * mirror)
    real_sum = jnp.zeros(below.shape, jnp.float32)
    imag_sum = jnp.zeros(below.shape, jnp.float32)
    for first_sign in (-1.0, 1.0):
        for second_sign in (-1.0, 1.0):
            delta_x = target_x - (source_x + first_sign * QUAD_OFFSET * halfsize)
            delta_y = target_y - (source_y + second_sign * QUAD_OFFSET * halfsize)
            planar = delta_x * delta_x + delta_y * delta_y + halfsq
            direct = lax.rsqrt(planar + below * below)
            image = lax.rsqrt(planar + mirror * mirror)
            phase = WAVE_NUMBER * jnp.sqrt(planar)
            wave_amp = depth_factor * lax.rsqrt(1.0 + phase)
            real_sum = real_sum + direct + image + wave_amp * jnp.cos(phase)
            imag_sum = imag_sum + wave_amp * jnp.sin(phase)
    same = col_panels[:, None] == row_panels[None, :]
    real_part = 0.25 * areas * real_sum + jnp.where(same, col_geometry[5][:, None], 0.0)
    imag_part = 0.25 * areas * imag_sum + jnp.where(same, col_geometry[6][:, None], 0.0)
    return (real_part, imag_part)


def assemble(real_part, imag_part):
    return jnp.stack(
        [jnp.stack([real_part, imag_part], 1), jnp.stack([-imag_part, real_part], 1)], 1
    )


def matmul(left, right):
    return jnp.dot(left, right, precision=lax.Precision.HIGHEST)


def leaf_factor(block):
    count = block.shape[0]
    positions = jnp.arange(count, dtype=jnp.int32)
    matrix = block
    for column in range(count):
        row_vals = matrix[column]
        col_vals = matrix[:, column]
        pivot_val = row_vals[column]
        later = positions > column
        factors = jnp.where(later, col_vals / pivot_val, 0.0)
        matrix = matrix - factors[:, None] * jnp.where(later, row_vals, 0.0)[None, :]
        placed = later[:, None] & (positions == column)[None, :]
        matrix = jnp.where(placed, factors[:, None], matrix)
    return matrix


def nilpotent_inverse(strict):
    count = strict.shape[0]
    identity = jnp.eye(count, dtype=jnp.float32)
    result = identity - strict
    power = matmul(strict, strict)
    while count > 2:
        result = matmul(result, identity + power)
        power = matmul(power, power)
        count = count // 2
    return result


def factor(matrix):
    count = matrix.shape[0]
    if count <= 16:
        packed = leaf_factor(matrix)
        identity = jnp.eye(count, dtype=jnp.float32)
        lower_all = jnp.tril(packed, -1) + identity
        upper_all = jnp.triu(packed)
        diagonal = jnp.diagonal(packed)
        lower_inv = nilpotent_inverse(jnp.tril(packed, -1))
        scaled = jnp.triu(packed, 1) / diagonal[:, None]
        upper_inv = nilpotent_inverse(scaled) / diagonal[None, :]
        return (lower_all, upper_all, lower_inv, upper_inv)
    half = count // 2
    lower_one, upper_one, lower_inv_one, upper_inv_one = factor(matrix[:half, :half])
    upper_side = matmul(lower_inv_one, matrix[:half, half:])
    lower_side = matmul(matrix[half:, :half], upper_inv_one)
    schur = matrix[half:, half:] - matmul(lower_side, upper_side)
    lower_two, upper_two, lower_inv_two, upper_inv_two = factor(schur)
    zeros_top = jnp.zeros((half, count - half), jnp.float32)
    lower_all = jnp.concatenate(
        [jnp.concatenate([lower_one, zeros_top], 1), jnp.concatenate([lower_side, lower_two], 1)], 0
    )
    upper_all = jnp.concatenate(
        [jnp.concatenate([upper_one, upper_side], 1), jnp.concatenate([zeros_top.T, upper_two], 1)],
        0,
    )
    lower_corner = -matmul(lower_inv_two, matmul(lower_side, lower_inv_one))
    upper_corner = -matmul(upper_inv_one, matmul(upper_side, upper_inv_two))
    lower_inv = jnp.concatenate(
        [
            jnp.concatenate([lower_inv_one, zeros_top], 1),
            jnp.concatenate([lower_corner, lower_inv_two], 1),
        ],
        0,
    )
    upper_inv = jnp.concatenate(
        [
            jnp.concatenate([upper_inv_one, upper_corner], 1),
            jnp.concatenate([zeros_top.T, upper_inv_two], 1),
        ],
        0,
    )
    return (lower_all, upper_all, lower_inv, upper_inv)


def pivot_rows(real_part, imag_part, pivots):
    wide_real = jnp.repeat(real_part, 2, axis=1)
    wide_imag = jnp.repeat(imag_part, 2, axis=1)
    swapped = (pivots % 2 == 1)[None, :]
    first_col = jnp.where(swapped, wide_imag, wide_real)
    second_col = jnp.where(swapped, wide_real, -wide_imag)
    return jnp.stack([first_col, second_col], 1).reshape(2 * real_part.shape[0], pivots.shape[0])


def body(panels, slab_ids, pivots):
    col_count = lax.axis_size("pcol")
    pcol_index = lax.axis_index("pcol")
    prow_index = lax.axis_index("prow")
    local_count = panels.shape[1]
    row_geometry = lax.all_gather(panels, "pcol", axis=1, tiled=True)
    row_count = row_geometry.shape[1]
    row_panels = prow_index * row_count + jnp.arange(row_count, dtype=jnp.int32)
    local_panels = (prow_index * col_count + pcol_index) * local_count + jnp.arange(
        local_count, dtype=jnp.int32
    )
    selector = (slab_ids[:, None] == local_panels[None, :]).astype(jnp.float32)
    picked = jnp.dot(panels, selector.T, precision=lax.Precision.HIGHEST)
    slab_geometry = lax.psum(picked, ("prow", "pcol"))
    slab_count = slab_ids.shape[0]
    pair_rows = pivots.shape[0]
    pivot_count = pair_rows // 2
    tile_width = slab_count // (col_count * col_count)
    panel_tiles = pivot_count // (tile_width * col_count)
    split_at = panel_tiles * tile_width
    own_geometry = lax.dynamic_slice_in_dim(
        slab_geometry.reshape(7, col_count, col_count, tile_width), pcol_index, 1, 2
    ).reshape(7, col_count * tile_width)
    own_panels = lax.dynamic_slice_in_dim(
        slab_ids.reshape(col_count, col_count, tile_width), pcol_index, 1, 1
    ).reshape(col_count * tile_width)
    head_geometry = jnp.concatenate([slab_geometry[:, :pivot_count], own_geometry[:, split_at:]], 1)
    head_panels = jnp.concatenate([slab_ids[:pivot_count], own_panels[split_at:]])
    real_part, imag_part = influence(
        slab_geometry[:, :pivot_count], slab_ids[:pivot_count], head_geometry, head_panels
    )
    pivot_block = pivot_rows(real_part, imag_part, pivots)
    leading = pivot_block[:pair_rows].T
    beside = pivot_block[pair_rows:].T
    lower_factor, upper_factor, lower_inverse, upper_inverse = factor(leading)
    upper_right = matmul(lower_inverse, beside)
    coupling = matmul(upper_inverse, upper_right)
    tile_base = (
        jnp.arange(col_count, dtype=jnp.int32)[:, None] * col_count + pcol_index
    ) * tile_width + jnp.arange(tile_width, dtype=jnp.int32)[None, :]
    own_columns = (
        2 * tile_base[:, :, None] + jnp.arange(2, dtype=jnp.int32)[None, None, :]
    ).reshape(-1)
    panel_columns = own_columns[: 2 * split_at]
    packed = jnp.tril(lower_factor, -1) + upper_factor
    head = jnp.concatenate([jnp.take(packed, panel_columns, axis=1), upper_right], 1).T.reshape(
        1, col_count, tile_width, 2, pair_rows
    )
    weights_lower = jnp.take(upper_inverse, panel_columns, axis=1)
    real_rows, imag_rows = influence(row_geometry, row_panels, own_geometry, own_panels)
    owned = assemble(real_rows, imag_rows).reshape(col_count * tile_width * 2, 2 * row_count)
    own_lower = owned[: 2 * split_at]
    own_trail = owned[2 * split_at :]
    contract = (((0,), (0,)), ((), ()))
    source = np.arange(col_count)[:, None, None, None]
    tile_pos = np.arange(panel_tiles)[None, :, None, None]
    inner = np.arange(tile_width)[None, None, :, None]
    parity = np.arange(2)[None, None, None, :]
    order = (2 * ((tile_pos * col_count + source) * tile_width + inner) + parity).reshape(-1)
    coefficients = jnp.concatenate([weights_lower[order], coupling[order]], 1)
    initial = jnp.zeros((coefficients.shape[1], 2 * row_count), jnp.float32)
    piece = lax.all_gather(own_lower, "pcol", axis=0, tiled=True)
    part = lax.slice_in_dim(coefficients, 0, piece.shape[0], axis=0)
    product = initial + lax.dot_general(part, piece, contract, precision=lax.Precision.HIGHEST)
    lower_out = product[: 2 * split_at].reshape(1, panel_tiles, tile_width, 2, 2, row_count)
    trail_out = (own_trail - product[2 * split_at :]).reshape(
        1, col_count - panel_tiles, tile_width, 2, 2, row_count
    )
    return (head, lower_out, trail_out)


def solution(mesh):
    placed = (P(None, ("prow", "pcol")), P(), P())
    return jax.shard_map(
        body,
        mesh=mesh,
        in_specs=placed,
        out_specs=(
            P("pcol", None, None, None, None),
            P("pcol", None, None, None, None, "prow"),
            P("pcol", None, None, None, None, "prow"),
        ),
        check_vma=False,
    )
```

profile of v0, /device:TPU:0, one launch (start us, length us, event | category | flops | bytes accessed | tf_op | source)
XLA Modules:
  0.0 1395.0 jit_solution(4944878906397128388)
XLA Ops:
  8.1 6.7 all_gather.6
  14.8 2.6 fusion.35
  17.4 41.0 %psum.7 = f32[7,1024]{1,0:T(8,128)S(1)} all-reduce(f32[7,1024]{1,0:T(8,128)S(1)} %fusion.35), channel_id=1, replica_groups=mesh['prow'=8,'pcol'=4] {'prow','pcol'}, use_global_device_ids=true, to_apply=%region_0.0 | all-reduce | flops 7168 | bytes 57344 | tf_op jit(solution)/shard_map/psum | solution.py:148
  59.4 77.8 %fusion.5 = (f32[256,1,4096]{2,0,1:T(8,128)S(1)}, f32[256,1,4096]{2,0,1:T(8,128)}, f32[256,1,4096]{2,0,1:T(8,128)}) fusion(f32[256]{0:T(256)S(1)} %broadcast_in_dim.8570, s32[4096]{0:T(1024)S(1)} %iota_add_fusion.1, f32[256]{0:T(256)S(1)} %add.2473, f32[256]{0:T(256)S(1)} %add.2463, f32[256]{0:T(256)S(1)} %sub.2698, f32[4096]{0:T(1024)S(1)} %bitcast.2390, ...), kind=kLoop, calls=%fused_computation.49 | loop fusion | flops 75497472 | bytes 12658688 | tf_op jit(solution)/shard_map/add | solution.py:39
  137.3 5.8 maximum_bitcast_fusion
  143.6 2.7 copy-done
  146.3 2.5 copy-done.1
  148.8 5.2 copy.82
  154.1 7.5 copy.90
  163.8 8.4 fusion.101
  174.2 1.7 reshape.4224
  175.9 2.2 broadcast_select_fusion
  179.6 2.0 slice.6211
  184.9 1.5 fusion.1157
  220.1 1.5 fusion.1124
  477.9 1.5 convert_add_fusion.119
  509.5 1.5 convert_add_fusion.114
  571.6 1.5 fusion.2678
  575.0 1.5 convert_add_fusion.104
  612.5 1.5 convert_add_fusion.99
  644.8 1.5 convert_add_fusion.94
  724.1 1.5 fusion.133
  725.6 1.5 fusion.135
  1169.7 1.7 copy.71
  1172.3 1.4 concatenate.1510
  1173.7 1.3 concatenate.1511
  1176.6 1.6 copy.69
  1178.1 1.5 concatenate.1509
  1179.6 1.8 copy.72
  1181.5 1.8 copy.70
  1183.3 1.5 slice.7858
  1185.4 1.4 slice.7860
  1237.1 4.3 fusion.39
  1251.8 1.5 gather_fusion.34
  1254.9 1.8 select_bitcast_fusion
  1256.8 1.6 gather_fusion.32
  1262.3 2.6 fusion.42
  1264.9 1.8 fusion.2779
  1266.8 1.6 gather_fusion.33
  1268.4 1.6 reshape.4225
  1270.0 10.9 pad_maximum_fusion
  1281.0 22.3 %copy.83 = f32[192,2,2,4096]{3,2,1,0:T(2,128)} copy(f32[192,2,2,4096]{3,0,2,1:T(8,128)} %pad_maximum_fusion) | data formatting | bytes 25165824 | tf_op jit(solution)/shard_map/slice | solution.py:187
  1303.3 21.6 %copy.91 = f32[48,8,2,4096]{3,1,2,0:T(8,128)} copy(f32[48,8,2,4096]{3,2,1,0:T(2,128)} %bitcast.2351) | data formatting | bytes 25165824
  1325.0 32.3 %fusion.77 = f32[512,8192]{1,0:T(8,128)S(1)} fusion(f32[512,8192]{1,0:T(8,128)} %all-gather.2.cloned.1.call-done, f32[512,384]{1,0:T(8,128)S(1)} %gather_fusion.33, f32[512,128]{1,0:T(8,128)S(1)} %copy-done.6), kind=kOutput, calls=%fused_computation.355 | convolution fusion | flops 25770065920 | bytes 34603008 | tf_op jit(solution)/shard_map/dot_general | solution.py:198
  1357.2 2.3 slice.9608
  1359.5 5.0 slice_subtract_fusion
  1364.6 6.6 reshape.4226
  1371.1 16.9 %reshape.4227 = f32[1,3,64,2,2,4096]{5,4,3,2,1,0:T(2,128)} reshape(f32[384,8192]{1,0:T(8,128)} %slice_subtract_fusion) | data formatting | bytes 25165824 | tf_op jit(solution)/shard_map/reshape | solution.py:200
  (3330 shorter events, 1041.5 us)
Async XLA Ops:
  7.2 1317.8 %all-gather.2.cloned.1.call-start = ((), (), s32[]{:S(2)}) async-start(), calls=%async_computation | async-start | bytes 20971520 | tf_op jit(solution)/shard_map/all_gather | solution.py:196
  163.2 274.2 %copy-start.36 = (pred[16]{0:T(512)(128)(4,1)}, pred[16]{0:T(512)(128)(4,1)S(1)}, u32[]{:S(2)}) copy-start(pred[16]{0:T(512)(128)(4,1)S(1)} %get-tuple-element.168) | copy-start | bytes 52
  163.2 274.2 %copy-start.41 = (pred[16]{0:T(512)(128)(4,1)}, pred[16]{0:T(512)(128)(4,1)S(1)}, u32[]{:S(2)}) copy-start(pred[16]{0:T(512)(128)(4,1)S(1)} %get-tuple-element.169) | copy-start | bytes 52
  182.9 132.6 %copy-start.3 = (f32[512,512]{0,1:T(8,128)S(1)}, f32[512,512]{0,1:T(8,128)}, u32[]{:S(2)}) copy-start(f32[512,512]{0,1:T(8,128)} %copy.65) | copy-start | bytes 3145732
  223.8 501.8 %copy-start.26 = (f32[16,16]{1,0:T(8,128)}, f32[16,16]{1,0:T(8,128)S(1)}, u32[]{:S(2)}) copy-start(f32[16,16]{1,0:T(8,128)S(1)} %convolution_divide_fusion.31) | copy-start | bytes 3076
  254.4 193.3 %copy-start.80 = (f32[16,32]{1,0:T(8,128)}, f32[16,32]{1,0:T(8,128)S(1)}, u32[]{:S(2)}) copy-start(f32[16,32]{1,0:T(8,128)S(1)} %concatenate.1171) | copy-start | bytes 6148
  254.5 122.6 %copy-start.83 = (f32[16,16]{1,0:T(8,128)}, f32[16,16]{1,0:T(8,128)S(1)}, u32[]{:S(2)}) copy-start(f32[16,16]{1,0:T(8,128)S(1)} %convolution_negate_fusion.61) | copy-start | bytes 3076
  257.1 123.1 %copy-start.132 = (f32[32,32]{1,0:T(8,128)}, f32[32,32]{1,0:T(8,128)S(1)}, u32[]{:S(2)}) copy-start(f32[32,32]{1,0:T(8,128)S(1)} %fusion.347) | copy-start | bytes 12292
  314.1 411.5 %copy-start.32 = (f32[32,64]{1,0:T(8,128)}, f32[32,64]{1,0:T(8,128)S(1)}, u32[]{:S(2)}) copy-start(f32[32,64]{1,0:T(8,128)S(1)} %concatenate.1186) | copy-start | bytes 24580
  314.9 410.7 %copy-start.34 = (f32[32,32]{1,0:T(8,128)}, f32[32,32]{1,0:T(8,128)S(1)}, u32[]{:S(2)}) copy-start(f32[32,32]{1,0:T(8,128)S(1)} %convolution_negate_fusion.29) | copy-start | bytes 12292
  315.8 131.7 %copy-start.46 = (f32[64,64]{1,0:T(8,128)}, f32[64,64]{1,0:T(8,128)S(1)}, u32[]{:S(2)}) copy-start(f32[64,64]{1,0:T(8,128)S(1)} %fusion.272) | copy-start | bytes 49156
  316.0 132.0 %copy-start.66 = (f32[64,64]{1,0:T(8,128)}, f32[64,64]{1,0:T(8,128)S(1)}, u32[]{:S(2)}) copy-start(f32[64,64]{1,0:T(8,128)S(1)} %fusion.274) | copy-start | bytes 49156
  380.5 67.2 %copy-start.84 = (f32[16,16]{1,0:T(8,128)S(1)}, f32[16,16]{1,0:T(8,128)}, u32[]{:S(2)}) copy-start(f32[16,16]{1,0:T(8,128)} %copy-done.83) | copy-start | bytes 3076
  452.2 66.0 %copy-start.11 = (f32[128,128]{0,1:T(8,128)}, f32[128,128]{0,1:T(8,128)S(1)}, u32[]{:S(2)}) copy-start(f32[128,128]{0,1:T(8,128)S(1)} %fusion.192) | copy-start | bytes 196612
  453.3 89.6 %copy-start.37 = (pred[16]{0:T(512)(128)(4,1)S(1)}, pred[16]{0:T(512)(128)(4,1)}, u32[]{:S(2)}) copy-start(pred[16]{0:T(512)(128)(4,1)} %copy-done.36) | copy-start | bytes 52
  453.3 89.5 %copy-start.42 = (pred[16]{0:T(512)(128)(4,1)S(1)}, pred[16]{0:T(512)(128)(4,1)}, u32[]{:S(2)}) copy-start(pred[16]{0:T(512)(128)(4,1)} %copy-done.41) | copy-start | bytes 52
  483.1 64.6 %copy-start.89 = (f32[16,16]{1,0:T(8,128)}, f32[16,16]{1,0:T(8,128)S(1)}, u32[]{:S(2)}) copy-start(f32[16,16]{1,0:T(8,128)S(1)} %convolution_divide_fusion.23) | copy-start | bytes 3076
  543.8 134.4 %copy-start.38 = (pred[16]{0:T(512)(128)(4,1)S(1)}, pred[16]{0:T(512)(128)(4,1)}, u32[]{:S(2)}) copy-start(pred[16]{0:T(512)(128)(4,1)} %copy-done.36) | copy-start | bytes 52
  543.8 134.4 %copy-start.43 = (pred[16]{0:T(512)(128)(4,1)S(1)}, pred[16]{0:T(512)(128)(4,1)}, u32[]{:S(2)}) copy-start(pred[16]{0:T(512)(128)(4,1)} %copy-done.41) | copy-start | bytes 52
  586.3 128.3 %copy-start.90 = (f32[16,16]{1,0:T(8,128)S(1)}, f32[16,16]{1,0:T(8,128)}, u32[]{:S(2)}) copy-start(f32[16,16]{1,0:T(8,128)} %copy-done.89) | copy-start | bytes 3076
  608.0 106.6 %copy-start.112 = (f32[32,32]{1,0:T(8,128)S(1)}, f32[32,32]{1,0:T(8,128)}, u32[]{:S(2)}) copy-start(f32[32,32]{1,0:T(8,128)} %copy-done.111) | copy-start | bytes 12292
  608.0 111.0 %copy-start.81 = (f32[16,32]{1,0:T(8,128)S(1)}, f32[16,32]{1,0:T(8,128)}, u32[]{:S(2)}) copy-start(f32[16,32]{1,0:T(8,128)} %copy-done.80) | copy-start | bytes 6148
  608.0 111.0 %copy-start.85 = (f32[16,16]{1,0:T(8,128)S(1)}, f32[16,16]{1,0:T(8,128)}, u32[]{:S(2)}) copy-start(f32[16,16]{1,0:T(8,128)} %copy-done.83) | copy-start | bytes 3076
  681.2 72.1 %copy-start.151 = (f32[16,32]{1,0:T(8,128)}, f32[16,32]{1,0:T(8,128)S(1)}, u32[]{:S(2)}) copy-start(f32[16,32]{1,0:T(8,128)S(1)} %concatenate.1293) | copy-start | bytes 6148
  720.2 82.6 %copy-start.91 = (f32[16,16]{1,0:T(8,128)}, f32[16,16]{1,0:T(8,128)S(1)}, u32[]{:S(2)}) copy-start(f32[16,16]{1,0:T(8,128)S(1)} %fusion.2696) | copy-start | bytes 3076
  721.1 64.8 %copy-start.153 = (f32[16,16]{1,0:T(8,128)}, f32[16,16]{1,0:T(8,128)S(1)}, u32[]{:S(2)}) copy-start(f32[16,16]{1,0:T(8,128)S(1)} %convolution_negate_fusion.46) | copy-start | bytes 3076
  752.6 94.6 %copy-start.5 = (f32[256,256]{1,0:T(8,128)S(1)}, f32[256,256]{1,0:T(8,128)}, u32[]{:S(2)}) copy-start(f32[256,256]{1,0:T(8,128)} %copy-done.4) | copy-start | bytes 786436
  754.8 209.4 %copy-start.24 = (f32[16,16]{1,0:T(8,128)}, f32[16,16]{1,0:T(8,128)S(1)}, u32[]{:S(2)}) copy-start(f32[16,16]{1,0:T(8,128)S(1)} %convolution_divide_fusion.15) | copy-start | bytes 3076
  783.5 180.7 %copy-start.51 = (f32[16,32]{1,0:T(8,128)}, f32[16,32]{1,0:T(8,128)S(1)}, u32[]{:S(2)}) copy-start(f32[16,32]{1,0:T(8,128)S(1)} %concatenate.1307) | copy-start | bytes 6148
  784.3 179.9 %copy-start.53 = (f32[16,16]{1,0:T(8,128)}, f32[16,16]{1,0:T(8,128)S(1)}, u32[]{:S(2)}) copy-start(f32[16,16]{1,0:T(8,128)S(1)} %convolution_negate_fusion.45) | copy-start | bytes 3076
  785.9 119.2 %copy-start.123 = (f32[32,32]{1,0:T(8,128)}, f32[32,32]{1,0:T(8,128)S(1)}, u32[]{:S(2)}) copy-start(f32[32,32]{1,0:T(8,128)S(1)} %fusion.329) | copy-start | bytes 12292
  814.5 115.3 %copy-start.39 = (pred[16]{0:T(512)(128)(4,1)S(1)}, pred[16]{0:T(512)(128)(4,1)}, u32[]{:S(2)}) copy-start(pred[16]{0:T(512)(128)(4,1)} %copy-done.36) | copy-start | bytes 52
  814.5 115.3 %copy-start.44 = (pred[16]{0:T(512)(128)(4,1)S(1)}, pred[16]{0:T(512)(128)(4,1)}, u32[]{:S(2)}) copy-start(pred[16]{0:T(512)(128)(4,1)} %copy-done.41) | copy-start | bytes 52
  846.0 118.2 %copy-start.28 = (f32[32,64]{1,0:T(8,128)}, f32[32,64]{1,0:T(8,128)S(1)}, u32[]{:S(2)}) copy-start(f32[32,64]{1,0:T(8,128)S(1)} %concatenate.1322) | copy-start | bytes 24580
  847.2 117.0 %copy-start.30 = (f32[32,32]{1,0:T(8,128)}, f32[32,32]{1,0:T(8,128)S(1)}, u32[]{:S(2)}) copy-start(f32[32,32]{1,0:T(8,128)S(1)} %convolution_negate_fusion.21) | copy-start | bytes 12292
  847.5 115.0 %copy-start.55 = (f32[64,64]{1,0:T(8,128)}, f32[64,64]{1,0:T(8,128)S(1)}, u32[]{:S(2)}) copy-start(f32[64,64]{1,0:T(8,128)S(1)} %fusion.260) | copy-start | bytes 49156
  847.7 115.3 %copy-start.68 = (f32[64,64]{1,0:T(8,128)}, f32[64,64]{1,0:T(8,128)S(1)}, u32[]{:S(2)}) copy-start(f32[64,64]{1,0:T(8,128)S(1)} %fusion.262) | copy-start | bytes 49156
  962.3 114.1 %copy-start.70 = (f32[64,128]{1,0:T(8,128)}, f32[64,128]{1,0:T(8,128)S(1)}, u32[]{:S(2)}) copy-start(f32[64,128]{1,0:T(8,128)S(1)} %concatenate.1355) | copy-start | bytes 98308
  963.8 114.5 %copy-start.72 = (f32[64,64]{1,0:T(8,128)}, f32[64,64]{1,0:T(8,128)S(1)}, u32[]{:S(2)}) copy-start(f32[64,64]{1,0:T(8,128)S(1)} %convolution_negate_fusion.9) | copy-start | bytes 49156
  964.2 115.1 %copy-start.12 = (f32[128,128]{0,1:T(8,128)}, f32[128,128]{0,1:T(8,128)S(1)}, u32[]{:S(2)}) copy-start(f32[128,128]{0,1:T(8,128)S(1)} %fusion.184) | copy-start | bytes 196612
  964.6 115.7 %copy-start.17 = (f32[128,128]{0,1:T(8,128)}, f32[128,128]{0,1:T(8,128)S(1)}, u32[]{:S(2)}) copy-start(f32[128,128]{0,1:T(8,128)S(1)} %fusion.186) | copy-start | bytes 196612
  992.1 115.7 %copy-start.87 = (f32[16,16]{1,0:T(8,128)}, f32[16,16]{1,0:T(8,128)S(1)}, u32[]{:S(2)}) copy-start(f32[16,16]{1,0:T(8,128)S(1)} %convolution_divide_fusion.7) | copy-start | bytes 3076
  1020.2 116.0 %copy-start.96 = (f32[16,32]{1,0:T(8,128)}, f32[16,32]{1,0:T(8,128)S(1)}, u32[]{:S(2)}) copy-start(f32[16,32]{1,0:T(8,128)S(1)} %concatenate.1371) | copy-start | bytes 6148
  1022.1 116.7 %copy-start.144 = (f32[32,32]{1,0:T(8,128)}, f32[32,32]{1,0:T(8,128)S(1)}, u32[]{:S(2)}) copy-start(f32[32,32]{1,0:T(8,128)S(1)} %fusion.323) | copy-start | bytes 12292
  1049.3 117.3 %copy-start.245 = (s32[4]{0:T(128)S(1)}, s32[4]{0:T(128)}, u32[]{:S(2)}) copy-start(s32[4]{0:T(128)} %add_multiply_fusion.5) | copy-start | bytes 52
  1078.4 90.1 %copy-start.114 = (f32[32,64]{1,0:T(8,128)}, f32[32,64]{1,0:T(8,128)S(1)}, u32[]{:S(2)}) copy-start(f32[32,64]{1,0:T(8,128)S(1)} %concatenate.1386) | copy-start | bytes 24580
  1080.0 88.5 %copy-start.109 = (f32[32,32]{1,0:T(8,128)}, f32[32,32]{1,0:T(8,128)S(1)}, u32[]{:S(2)}) copy-start(f32[32,32]{1,0:T(8,128)S(1)} %convolution_negate_fusion.17) | copy-start | bytes 12292
  1080.3 88.3 %copy-start.63 = (f32[64,64]{1,0:T(8,128)}, f32[64,64]{1,0:T(8,128)S(1)}, u32[]{:S(2)}) copy-start(f32[64,64]{1,0:T(8,128)S(1)} %fusion.254) | copy-start | bytes 49156
  (199 other events, 5177.3 us)
Sparse Core Ops, SparseCore 0:
  161.7 105.7 all-gather.1
where the time goes:
time: 1410 us; the launch traced here: 1400 us
  other arithmetic  669 us (47%)
  local copies, waits for them, and re-layouts  459 us (33%)
  matrix products  195 us (14%)
  blocking collectives  47.7 us (3%)
  between operations  23.6 us (2%)
    select_n x512, other arithmetic, leaf_factor(): factors = jnp.where(later, col_vals / pivot_val, 0.0)  414 us
    slice x512, local copies, waits for them, and re-layouts, leaf_factor(): pivot_val = row_vals[column]  303 us
    dot_general x603, matrix products, matmul(): return jnp.dot(left, right, precision=lax.Precision.HIGHEST)  160 us
    add x2, other arithmetic, influence(): 0.25 * areas * imag_sum + jnp.where(same, col_geometry[6][:, None], 0.0)  86.2 us
    select_n x480, other arithmetic, leaf_factor(): matrix = jnp.where(placed, factors[:, None], matrix)  68.4 us
    unnamed x494, local copies, waits for them, and re-layouts  41.8 us
    psum x1, blocking collectives, body(): slab_geometry = lax.psum(picked, ('prow', 'pcol'))  41 us
    dot_general x1, matrix products, body(): lax.dot_general(part, piece, contract, precision=lax.Precision.HIGHEST)  32.3 us
  transfers between devices with their start and end apart: 1, of which 0 were waited for; matrix products, arithmetic and copies ran while one was open for 82% of the time, Pallas kernels for 0%

commit v1 on v0

v1 whole, which is shorter than its diff:
```python
import jax
import jax.numpy as jnp
import numpy as np
from jax import lax
from jax.experimental import pallas as pl
from jax.experimental.pallas import tpu as pltpu
from jax.sharding import PartitionSpec as P

QUAD_OFFSET = 0.5773502691896258
WAVE_NUMBER = 6.0
BLOCK = 64


def fit_trig():
    nodes = 0.25 * (1.0 + np.cos(np.pi * (np.arange(400) + 0.5) / 400)) * 0.5
    root = np.sqrt(nodes)
    sine = np.sin(np.pi * root) / root * np.sqrt(2.0)
    cosine = np.cos(np.pi * root) * np.sqrt(2.0)
    powers = nodes[:, None] ** np.arange(5)[None, :]
    return (
        [float(c) for c in np.linalg.lstsq(powers, sine, rcond=None)[0]],
        [float(c) for c in np.linalg.lstsq(powers, cosine, rcond=None)[0]],
    )


SIN_COEF, COS_COEF = fit_trig()


def horner(coef, arg):
    total = coef[-1]
    for value in coef[-2::-1]:
        total = total * arg + value
    return total


def entries(tx, ty, tz, te, tid, left_x, right_x, left_y, right_y, halfsq, sz, se, area, sr, si, sid):
    below = tz - sz
    mirror = tz + sz
    below_sq = below * below
    mirror_sq = mirror * mirror
    squares_x = []
    squares_y = []
    for pos in (left_x, right_x):
        delta = tx - pos
        squares_x.append(delta * delta + halfsq)
    for pos in (left_y, right_y):
        delta = ty - pos
        squares_y.append(delta * delta)
    near = None
    wave_re = None
    wave_im = None
    for sq_x in squares_x:
        for sq_y in squares_y:
            planar = sq_x + sq_y
            both = lax.rsqrt(planar + below_sq) + lax.rsqrt(planar + mirror_sq)
            rho = planar * lax.rsqrt(planar)
            amp = lax.rsqrt(rho * WAVE_NUMBER + 1.0)
            turns = rho * (WAVE_NUMBER / (2.0 * np.pi))
            part = turns - jnp.round(turns)
            part_sq = part * part
            sine = part * horner(SIN_COEF, part_sq)
            cosine = horner(COS_COEF, part_sq)
            scaled = amp * sine
            re = amp - scaled * sine
            im = scaled * cosine
            near = both if near is None else near + both
            wave_re = re if wave_re is None else wave_re + re
            wave_im = im if wave_im is None else wave_im + im
    factor = te * se
    same = tid == sid
    real = area * (near + factor * wave_re) + jnp.where(same, sr, 0.0)
    imag = area * (factor * wave_im) + jnp.where(same, si, 0.0)
    return real, imag


def source_params(geometry, ids):
    offset = QUAD_OFFSET * geometry[4]
    zeros = jnp.zeros_like(offset)
    return jnp.stack(
        [
            geometry[0] - offset,
            geometry[0] + offset,
            geometry[1] - offset,
            geometry[1] + offset,
            geometry[4] * geometry[4],
            geometry[2],
            2.0 * WAVE_NUMBER * jnp.exp(WAVE_NUMBER * geometry[2]),
            0.25 * geometry[3],
            geometry[5],
            geometry[6],
            ids.astype(jnp.float32),
            zeros,
            zeros,
            zeros,
            zeros,
            zeros,
        ]
    )


def target_params(geometry, ids):
    zeros = jnp.zeros_like(geometry[0])
    return jnp.stack(
        [
            geometry[0],
            geometry[1],
            geometry[2],
            jnp.exp(WAVE_NUMBER * geometry[2]),
            ids.astype(jnp.float32),
            zeros,
            zeros,
            zeros,
        ]
    )


def matmul(left, right):
    return jnp.dot(left, right, precision=lax.Precision.HIGHEST, preferred_element_type=jnp.float32)


def cmul(ar, ai, br, bi):
    return matmul(ar, br) - matmul(ai, bi), matmul(ar, bi) + matmul(ai, br)


def invert_block(re, im, rec_r, rec_i):
    size = re.shape[0]
    wide = 2 * size
    rows = lax.broadcasted_iota(jnp.int32, (size, wide), 0)
    lanes = lax.broadcasted_iota(jnp.int32, (size, wide), 1)
    rows_one = lax.broadcasted_iota(jnp.int32, (size, 1), 0)
    eye = jnp.where(
        lax.broadcasted_iota(jnp.int32, (size, size), 0) == lax.broadcasted_iota(jnp.int32, (size, size), 1), 1.0, 0.0
    )
    start_r = jnp.concatenate([re, eye], 1)
    start_i = jnp.concatenate([im, jnp.zeros_like(eye)], 1)

    def step(col, carry):
        mr, mi = carry
        at_lane = lanes == col
        at_row = rows == col
        col_r = jnp.sum(jnp.where(at_lane, mr, 0.0), axis=1, keepdims=True)
        col_i = jnp.sum(jnp.where(at_lane, mi, 0.0), axis=1, keepdims=True)
        row_r = jnp.sum(jnp.where(at_row, mr, 0.0), axis=0, keepdims=True)
        row_i = jnp.sum(jnp.where(at_row, mi, 0.0), axis=0, keepdims=True)
        rec_r[pl.ds(col, 1), :] = row_r
        rec_i[pl.ds(col, 1), :] = row_i
        piv_r = jnp.sum(jnp.where(at_lane[:1], row_r, 0.0), axis=1, keepdims=True)
        piv_i = jnp.sum(jnp.where(at_lane[:1], row_i, 0.0), axis=1, keepdims=True)
        norm = 1.0 / (piv_r * piv_r + piv_i * piv_i)
        inv_r = piv_r * norm
        inv_i = -piv_i * norm
        num_r = jnp.where(rows_one == col, col_r - 1.0, col_r)
        f_r = num_r * inv_r - col_i * inv_i
        f_i = num_r * inv_i + col_i * inv_r
        later = lanes > col
        new_r = mr - (f_r * row_r - f_i * row_i)
        new_i = mi - (f_r * row_i + f_i * row_r)
        out_r = jnp.where(later, new_r, jnp.where(at_lane, f_r, mr))
        out_i = jnp.where(later, new_i, jnp.where(at_lane, f_i, mi))
        return out_r, out_i

    return lax.fori_loop(0, size, step, (start_r, start_i))


def factor_kernel(own_elim, own_trail, tgt, src, own, packed_r, packed_i, head_r, head_i, sol_r, sol_i, rec_r, rec_i, uin_r, uin_i):
    count = tgt.shape[0]
    width = count + own_trail
    for part in range(0, count, 32):
        targets = [tgt[part : part + 32, n : n + 1] for n in range(5)]
        sources = [src[n : n + 1, :] for n in range(11)]
        re, im = entries(*targets, *sources)
        packed_r[part : part + 32, :] = re
        packed_i[part : part + 32, :] = im
    size = BLOCK
    steps = count // size
    rows = lax.broadcasted_iota(jnp.int32, (size, size), 0)
    cols = lax.broadcasted_iota(jnp.int32, (size, size), 1)
    for step in range(steps):
        lo = step * size
        hi = lo + size
        fin_r, fin_i = invert_block(packed_r[lo:hi, lo:hi], packed_i[lo:hi, lo:hi], rec_r, rec_i)
        strict = rows > cols
        low_r = jnp.where(strict, fin_r[:, :size], 0.0)
        low_i = jnp.where(strict, fin_i[:, :size], 0.0)
        eye = jnp.where(rows == cols, 1.0, 0.0)
        uinv_r, uinv_i = cmul(fin_r[:, size:], fin_i[:, size:], low_r + eye, low_i)
        uinv_r = jnp.where(strict, 0.0, uinv_r)
        uinv_i = jnp.where(strict, 0.0, uinv_i)
        uin_r[lo:hi, :] = uinv_r
        uin_i[lo:hi, :] = uinv_i
        linv_r = rec_r[:, size:]
        linv_i = rec_i[:, size:]
        packed_r[lo:hi, lo:hi] = jnp.where(strict, low_r, rec_r[:, :size])
        packed_i[lo:hi, lo:hi] = jnp.where(strict, low_i, rec_i[:, :size])
        up_r, up_i = cmul(linv_r, linv_i, packed_r[lo:hi, hi:width], packed_i[lo:hi, hi:width])
        packed_r[lo:hi, hi:width] = up_r
        packed_i[lo:hi, hi:width] = up_i
        if hi < count:
            dn_r, dn_i = cmul(packed_r[hi:count, lo:hi], packed_i[hi:count, lo:hi], uinv_r, uinv_i)
            packed_r[hi:count, lo:hi] = dn_r
            packed_i[hi:count, lo:hi] = dn_i
            pr, pi = cmul(dn_r, dn_i, up_r, up_i)
            packed_r[hi:count, hi:width] = packed_r[hi:count, hi:width] - pr
            packed_i[hi:count, hi:width] = packed_i[hi:count, hi:width] - pi
    sel_rows = lax.broadcasted_iota(jnp.int32, (count, own_elim), 0)
    select = jnp.where(sel_rows == own[0:1, :], 1.0, 0.0)
    head_r[...] = matmul(packed_r[:, :count], select)
    head_i[...] = matmul(packed_i[:, :count], select)
    for step in range(steps - 1, -1, -1):
        lo = step * size
        hi = lo + size
        rhs_r = jnp.concatenate([select[lo:hi], packed_r[lo:hi, count:width]], 1)
        rhs_i = jnp.concatenate([jnp.zeros_like(select[lo:hi]), packed_i[lo:hi, count:width]], 1)
        if hi < count:
            pr, pi = cmul(
                packed_r[lo:hi, hi:count], packed_i[lo:hi, hi:count], sol_r[hi:count, :], sol_i[hi:count, :]
            )
            rhs_r = rhs_r - pr
            rhs_i = rhs_i - pi
        xr, xi = cmul(uin_r[lo:hi, :], uin_i[lo:hi, :], rhs_r, rhs_i)
        sol_r[lo:hi, :] = xr
        sol_i[lo:hi, :] = xi


def rows_kernel(own_elim, own_trail, count, tgt, src, whi, wlo, fix, lower, trail, ghi, glo, own_r, own_i):
    lanes = tgt.shape[1]
    targets = [tgt[n : n + 1, :] for n in range(5)]

    @pl.loop(0, count // 16)
    def _(group):
        base = pl.multiple_of(group * 16, 16)
        params = src[pl.ds(base, 16), :]
        re, im = entries(*targets, *[params[:, n : n + 1] for n in range(11)])
        for start, value in ((0, re), (count, im)):
            top = value.astype(jnp.bfloat16)
            where = pl.ds(pl.multiple_of(start + base, 16), 16)
            ghi[where, :] = top
            glo[where, :] = (value - top.astype(jnp.float32)).astype(jnp.bfloat16)

    @pl.loop(0, own_trail // 16)
    def _(group):
        base = pl.multiple_of(group * 16, 16)
        params = src[pl.ds(count + base, 16), :]
        re, im = entries(*targets, *[params[:, n : n + 1] for n in range(11)])
        own_r[pl.ds(base, 16), :] = re
        own_i[pl.ds(base, 16), :] = im

    def product(lo, hi):
        total = jnp.dot(whi[lo:hi, :], ghi[...], preferred_element_type=jnp.float32)
        total += jnp.dot(whi[lo:hi, :], glo[...], preferred_element_type=jnp.float32)
        total += jnp.dot(wlo[lo:hi, :], ghi[...], preferred_element_type=jnp.float32)
        return total

    width = own_elim + own_trail
    re = product(0, own_elim)
    im = product(width, width + own_elim)
    for b in range(2):
        fr = fix[:, 2 * b : 2 * b + 1]
        fi = fix[:, 2 * b + 1 : 2 * b + 2]
        lower[:, b, 0, :] = re * fr - im * fi
        lower[:, b, 1, :] = re * fi + im * fr
    re = own_r[...] - product(own_elim, width)
    im = own_i[...] - product(width + own_elim, 2 * width)
    trail[:, 0, 0, :] = re
    trail[:, 0, 1, :] = im
    trail[:, 1, 0, :] = -im
    trail[:, 1, 1, :] = re


def swap_rows(re, im, swapped):
    first = (jnp.where(swapped, im, re), jnp.where(swapped, re, -im))
    second = (jnp.where(swapped, re, im), jnp.where(swapped, -im, re))
    return first, second


def body(panels, slab_ids, pivots):
    col_count = lax.axis_size("pcol")
    pcol_index = lax.axis_index("pcol")
    prow_index = lax.axis_index("prow")
    local_count = panels.shape[1]
    row_geometry = lax.all_gather(panels, "pcol", axis=1, tiled=True)
    row_count = row_geometry.shape[1]
    row_panels = prow_index * row_count + jnp.arange(row_count, dtype=jnp.int32)
    local_panels = (prow_index * col_count + pcol_index) * local_count + jnp.arange(
        local_count, dtype=jnp.int32
    )
    selector = (slab_ids[:, None] == local_panels[None, :]).astype(jnp.float32)
    picked = jnp.dot(panels, selector.T, precision=lax.Precision.HIGHEST)
    slab_geometry = lax.psum(picked, ("prow", "pcol"))
    slab_count = slab_ids.shape[0]
    count = pivots.shape[0] // 2
    tile_width = slab_count // (col_count * col_count)
    panel_tiles = count // (tile_width * col_count)
    own_elim = panel_tiles * tile_width
    own_width = col_count * tile_width
    own_trail = own_width - own_elim
    own_geometry = lax.dynamic_slice_in_dim(
        slab_geometry.reshape(7, col_count, col_count, tile_width), pcol_index, 1, 2
    ).reshape(7, own_width)
    own_panels = lax.dynamic_slice_in_dim(
        slab_ids.reshape(col_count, col_count, tile_width), pcol_index, 1, 1
    ).reshape(own_width)
    src_geometry = jnp.concatenate([slab_geometry[:, :count], own_geometry[:, own_elim:]], 1)
    src_ids = jnp.concatenate([slab_ids[:count], own_panels[own_elim:]])
    src = source_params(src_geometry, src_ids)
    own_index = (
        (jnp.arange(panel_tiles, dtype=jnp.int32)[:, None] * col_count + pcol_index) * tile_width
        + jnp.arange(tile_width, dtype=jnp.int32)[None, :]
    ).reshape(-1)
    own_rows = jnp.broadcast_to(own_index[None, :], (8, own_elim))
    width = count + own_trail
    f32 = jnp.float32
    packed_r, packed_i, head_r, head_i, sol_r, sol_i = pl.pallas_call(
        lambda *refs: factor_kernel(own_elim, own_trail, *refs),
        out_shape=[jax.ShapeDtypeStruct((count, width), f32)] * 2
        + [jax.ShapeDtypeStruct((count, own_elim), f32)] * 2
        + [jax.ShapeDtypeStruct((count, own_width), f32)] * 2,
        scratch_shapes=[pltpu.VMEM((BLOCK, 2 * BLOCK), f32)] * 2 + [pltpu.VMEM((count, BLOCK), f32)] * 2,
        compiler_params=pltpu.CompilerParams(vmem_limit_bytes=32 * 1024 * 1024),
    )(target_params(slab_geometry[:, :count], slab_ids[:count]).T, src, own_rows)

    swapped = pivots[::2] % 2 == 1
    eye = jnp.eye(count, dtype=jnp.bool_)
    diag_r = jnp.sum(jnp.where(eye, packed_r[:, :count], 0.0), axis=1)
    diag_i = jnp.sum(jnp.where(eye, packed_i[:, :count], 0.0), axis=1)
    lam = jnp.where(swapped, diag_r, diag_i) / jnp.where(swapped, diag_i, diag_r)
    own_hot = own_index[:, None] == jnp.arange(count, dtype=jnp.int32)[None, :]
    own_lam = jnp.sum(jnp.where(own_hot, lam[None, :], 0.0), axis=1)
    own_swap = jnp.any(own_hot & swapped[None, :], axis=1)

    full_r = jnp.concatenate([head_r, packed_r[:, count:]], 1).T
    full_i = jnp.concatenate([head_i, packed_i[:, count:]], 1).T
    (a00, a01), (a10, a11) = swap_rows(full_r, full_i, swapped[None, :])
    u00, u01 = a00, a01
    u10 = a10 - lam[None, :] * a00
    u11 = a11 - lam[None, :] * a01
    k_lam = own_lam[:, None]
    k_swap = own_swap[:, None]

    def columns(c0, c1):
        first = jnp.where(k_swap, c1, c0)
        second = jnp.where(k_swap, c0, c1)
        return first + k_lam * second, second

    l00, l01 = columns(a00[:own_elim], a01[:own_elim])
    l10, l11 = columns(a10[:own_elim], a11[:own_elim])
    row_at = jnp.arange(count, dtype=jnp.int32)[None, :]
    is_low = row_at > own_index[:, None]
    is_diag = row_at == own_index[:, None]

    def merge(low, up):
        return jnp.concatenate([jnp.where(is_low, low, up[:own_elim]), up[own_elim:]], 0)

    h00 = merge(l00, u00)
    h01 = merge(l01, u01)
    h10 = merge(l10, u10)
    h10 = jnp.concatenate([jnp.where(is_diag, k_lam, h10[:own_elim]), h10[own_elim:]], 0)
    h11 = merge(l11, u11)
    head = jnp.stack([jnp.stack([h00, h10], 2), jnp.stack([h01, h11], 2)], 1).reshape(
        1, col_count, tile_width, 2, 2 * count
    )

    fix = jnp.stack(
        [
            jnp.where(own_swap, own_lam, 1.0),
            jnp.where(own_swap, 1.0, own_lam),
            jnp.where(own_swap, 1.0, 0.0),
            jnp.where(own_swap, 0.0, 1.0),
        ],
        1,
    )
    wt_r = sol_r.T
    wt_i = sol_i.T
    weights = jnp.concatenate([jnp.concatenate([wt_r, -wt_i], 1), jnp.concatenate([wt_i, wt_r], 1)], 0)
    top = lax.reduce_precision(weights, 8, 7)
    whi = top.astype(jnp.bfloat16)
    wlo = (weights - top).astype(jnp.bfloat16)
    tile = 512
    src_cols = src.T
    lower, trail = pl.pallas_call(
        lambda *refs: rows_kernel(own_elim, own_trail, count, *refs),
        grid=(row_count // tile,),
        in_specs=[
            pl.BlockSpec((8, tile), lambda i: (0, i)),
            pl.BlockSpec(src_cols.shape, lambda i: (0, 0)),
            pl.BlockSpec(whi.shape, lambda i: (0, 0)),
            pl.BlockSpec(wlo.shape, lambda i: (0, 0)),
            pl.BlockSpec(fix.shape, lambda i: (0, 0)),
        ],
        out_specs=[
            pl.BlockSpec((own_elim, 2, 2, tile), lambda i: (0, 0, 0, i)),
            pl.BlockSpec((own_trail, 2, 2, tile), lambda i: (0, 0, 0, i)),
        ],
        out_shape=[
            jax.ShapeDtypeStruct((own_elim, 2, 2, row_count), f32),
            jax.ShapeDtypeStruct((own_trail, 2, 2, row_count), f32),
        ],
        scratch_shapes=[
            pltpu.VMEM((2 * count, tile), jnp.bfloat16),
            pltpu.VMEM((2 * count, tile), jnp.bfloat16),
            pltpu.VMEM((own_trail, tile), f32),
            pltpu.VMEM((own_trail, tile), f32),
        ],
        compiler_params=pltpu.CompilerParams(vmem_limit_bytes=48 * 1024 * 1024),
    )(target_params(row_geometry, row_panels), src_cols, whi, wlo, fix)
    lower_out = lower.reshape(1, panel_tiles, tile_width, 2, 2, row_count)
    trail_out = trail.reshape(1, col_count - panel_tiles, tile_width, 2, 2, row_count)
    return (head, lower_out, trail_out)


def solution(mesh):
    placed = (P(None, ("prow", "pcol")), P(), P())
    return jax.shard_map(
        body,
        mesh=mesh,
        in_specs=placed,
        out_specs=(
            P("pcol", None, None, None, None),
            P("pcol", None, None, None, None, "prow"),
            P("pcol", None, None, None, None, "prow"),
        ),
        check_vma=False,
    )
```

time: 1410 us -> 190 us (0.13); the launches traced: 1400 us -> 189 us
  other arithmetic: 669 us -> 5.47 us
  local copies, waits for them, and re-layouts: 459 us -> 12.6 us
  matrix products: 195 us -> 2.64 us
  Pallas kernels: 0 us -> 120 us
  between operations: 23.6 us -> 0.94 us
    select_n x997 -> x2, other arithmetic: 488 us -> 0.09 us  [the longest x1 0.08 us: merge(): jnp.where(is_low, low, up[:own_elim])]
    slice x529 -> x12, local copies, waits for them, and re-layouts: 341 us -> 1.56 us  [the longest x1 0.9 us: body(): swapped = pivots[::2] % 2 == 1]
    dot_general x604 -> x0, matrix products: 192 us -> none  [the longest x603 160 us: matmul(): return jnp.dot(left, right, precision=lax.Precision.HIGHEST)]
    add x42 -> x1, other arithmetic: 120 us -> 0.01 us  [body(): (jnp.arange(panel_tiles, dtype=jnp.int32)[:, None] * col_count + pcol_ind...]
    pallas_call x0 -> x2, Pallas kernels: none -> 120 us  [the longest x1 75.1 us: body(): pl.pallas_call(lambda *refs: rows_kernel(own_elim, own_trail, count, *ref...]
    unnamed x494 -> x1, local copies, waits for them, and re-layouts: 41.8 us -> 3.89 us
    concatenate x63 -> x1, other arithmetic: 33.5 us -> 0.01 us  [body(): jnp.concatenate([slab_geometry[:, :count], own_geometry[:, own_elim:]], 1)]
    reshape x5 -> x0, local copies, waits for them, and re-layouts: 27.5 us -> none  [the longest x1 16.9 us: body(): (own_trail - product[2 * split_at:]).reshape(1, col_count - panel_tiles,...]
  transfers between devices with their start and end apart: 1 -> 0, of which waited for: 0 -> 0; matrix products, arithmetic and copies ran while one was open for 82% -> 0% of each run, Pallas kernels for 0% -> 0%
where the time goes in v1:
time: 190 us; the launch traced here: 189 us
  Pallas kernels  120 us (63%)
  blocking collectives  48.1 us (25%)
  local copies, waits for them, and re-layouts  12.6 us (7%)
  other arithmetic  5.47 us (3%)
  matrix products  2.64 us (1%)
    pallas_call x1, Pallas kernels, body(): pl.pallas_call(lambda *refs: rows_kernel(own_elim, own_trail, count, *ref...  75.1 us
    pallas_call x1, Pallas kernels, body(): pl.pallas_call(lambda *refs: factor_kernel(own_elim, own_trail, *refs), o...  44.5 us
    psum x1, blocking collectives, body(): slab_geometry = lax.psum(picked, ('prow', 'pcol'))  42.1 us
    all_gather x1, blocking collectives, body(): row_geometry = lax.all_gather(panels, 'pcol', axis=1, tiled=True)  6 us
    unnamed x1, local copies, waits for them, and re-layouts  3.89 us

profile of v1, /device:TPU:0, one launch (start us, length us, event | category | flops | bytes accessed | tf_op | source)
XLA Modules:
  0.0 189.4 jit_solution(511496119146865419)
XLA Ops:
  0.7 0.9 slice.108
  1.5 0.7 fusion.22
  2.2 0.8 reshape.139
  3.0 0.1 concatenate.47
  3.2 2.6 %fusion.4 = f32[7,1024]{1,0:T(8,128)S(1)} fusion(f32[7,1024]{1,0:T(8,128)} %param.3, s32[1024]{0:T(1024)S(1)} %iota_add_fusion, s32[1024]{0:T(1024)} %param.4), kind=kOutput, calls=%fused_computation.7 | convolution fusion | flops 89128960 | bytes 65536 | tf_op jit(solution)/shard_map/dot_general | solution.py:288
  5.8 42.1 %psum.7 = f32[7,1024]{1,0:T(8,128)S(1)} all-reduce(f32[7,1024]{1,0:T(8,128)S(1)} %fusion.4), channel_id=1, replica_groups=mesh['prow'=8,'pcol'=4] {'prow','pcol'}, use_global_device_ids=true, to_apply=%region_1.2 | all-reduce | flops 7168 | bytes 57344 | tf_op jit(solution)/shard_map/psum | solution.py:289
  48.0 0.1 reshape.137
  48.1 0.1 dynamic-slice_reduce_fusion
  48.1 0.1 reshape.138
  48.2 0.1 slice.140
  48.4 0.1 stack.71.refs_1_
  48.5 0.1 copy.30
  48.6 6.0 %all_gather.3 = f32[7,4096]{1,0:T(8,128)S(1)} all-gather(f32[7,1024]{1,0:T(8,128)} %param.3), channel_id=1, replica_groups=mesh['prow'=8,'pcol'=4] {'pcol'}, dimensions={1}, use_global_device_ids=true | all-gather | bytes 143360 | tf_op jit(solution)/shard_map/all_gather | solution.py:281
  54.7 0.1 stack.82.refs_0_
  54.8 0.1 copy.33
  54.9 44.5 %shard_map.58 = (f32[256,448]{1,0:T(8,128)S(1)}, f32[256,448]{1,0:T(8,128)S(1)}, f32[256,64]{1,0:T(8,128)S(1)}, f32[256,64]{1,0:T(8,128)S(1)}, f32[256,256]{1,0:T(8,128)S(1)}, /*index=5*/f32[256,256]{1,0:T(8,128)S(1)}) custom-call(f32[256,8]{1,0:T(8,128)S(1)} %bitcast.61, f32[16,448]{1,0:T(8,128)S(1)} %stack.71.refs_1_, s32[8,64]{1,0:T(8,128)S(1)} %broadcast_in_dim.90.refs_2_), custom_call_target="tpu_custom_call" | custom-call | tf_op jit(solution)/shard_map/pallas_call | solution.py:313
  99.5 0.2 select_reduce_fusion
  99.7 0.1 select_reduce_fusion.2
  99.8 0.1 fusion.11
  99.9 0.1 copy.36.refs_4_
  100.0 0.1 copy.35
  100.2 0.1 copy.34
  100.3 0.1 fusion.7
  100.5 0.3 multiply_subtract_fusion.1
  100.8 0.1 add_select_fusion
  100.9 0.1 slice.147
  101.0 0.1 slice.150
  101.1 0.1 slice.148
  101.3 0.1 slice.143
  101.4 0.1 maximum_bitcast_fusion.3
  101.6 0.1 maximum_bitcast_fusion.5
  101.7 0.1 maximum_bitcast_fusion.2
  101.9 0.4 copy.31
  102.3 0.1 maximum_bitcast_fusion.4
  102.5 1.2 copy.32
  103.7 1.9 stack.79
  105.5 1.8 stack.75
  107.3 3.1 %pad_maximum_fusion = f32[1,4,64,2,512]{2,1,4,3,0:T(4,128)} fusion(f32[1,4,64,1,512]{2,1,4,3,0:T(4,128)S(1)} %stack.79, f32[1,4,64,1,512]{2,1,4,3,0:T(4,128)} %stack.75), kind=kLoop, calls=%fused_computation.2 | loop fusion | flops 262144 | bytes 2097152 | tf_op jit(solution)/shard_map/stack | solution.py:359
  110.4 3.9 %copy.37 = f32[1,4,64,2,512]{4,3,2,1,0:T(2,128)} copy(f32[1,4,64,2,512]{2,1,4,3,0:T(4,128)} %pad_maximum_fusion) | data formatting | bytes 2097152
  114.3 75.1 %shard_map.59 = (f32[64,2,2,4096]{3,2,1,0:T(2,128)}, f32[192,2,2,4096]{3,2,1,0:T(2,128)}) custom-call(f32[8,4096]{1,0:T(8,128)S(1)} %stack.82.refs_0_, f32[448,16]{1,0:T(8,128)S(1)} %bitcast.60, bf16[512,512]{1,0:T(8,128)(2,1)S(1)} %get-tuple-element.45.refs_2_, bf16[512,512]{1,0:T(8,128)(2,1)S(1)} %get-tuple-element.44.refs_3_, f32[64,4]{1,0:T(8,128)S(1)} %copy.36.refs_4_), custom_call_target="tpu_custom_call" | custom-call | tf_op jit(solution)/shard_map/pallas_call | solution.py:380
  (30 shorter events, 0.4 us)

commit v2 on v1

--- a/solution.py
+++ b/solution.py
@@ -224,13 +224,22 @@
 
 def rows_kernel(own_elim, own_trail, count, tgt, src, whi, wlo, fix, lower, trail, ghi, glo, own_r, own_i):
     lanes = tgt.shape[1]
-    targets = [tgt[n : n + 1, :] for n in range(5)]
+    def halves(base):
+        pieces = []
+        for half in range(2):
+            params = src[pl.ds(pl.multiple_of(base + 8 * half, 8), 8), :]
+            sources = [jnp.broadcast_to(params[:, n : n + 1], (8, 256)) for n in range(11)]
+            parts = []
+            for lo in range(0, lanes, 256):
+                targets = [tgt[n : n + 1, lo : lo + 256] for n in range(5)]
+                parts.append(entries(*targets, *sources))
+            pieces.append([jnp.concatenate([part[c] for part in parts], 1) for c in range(2)])
+        return [jnp.concatenate([piece[c] for piece in pieces], 0) for c in range(2)]
 
     @pl.loop(0, count // 16)
     def _(group):
         base = pl.multiple_of(group * 16, 16)
-        params = src[pl.ds(base, 16), :]
-        re, im = entries(*targets, *[params[:, n : n + 1] for n in range(11)])
+        re, im = halves(base)
         for start, value in ((0, re), (count, im)):
             top = value.astype(jnp.bfloat16)
             where = pl.ds(pl.multiple_of(start + base, 16), 16)
@@ -240,8 +249,7 @@
     @pl.loop(0, own_trail // 16)
     def _(group):
         base = pl.multiple_of(group * 16, 16)
-        params = src[pl.ds(count + base, 16), :]
-        re, im = entries(*targets, *[params[:, n : n + 1] for n in range(11)])
+        re, im = halves(count + base)
         own_r[pl.ds(base, 16), :] = re
         own_i[pl.ds(base, 16), :] = im
 
@@ -286,7 +294,7 @@
     )
     selector = (slab_ids[:, None] == local_panels[None, :]).astype(jnp.float32)
     picked = jnp.dot(panels, selector.T, precision=lax.Precision.HIGHEST)
-    slab_geometry = lax.psum(picked, ("prow", "pcol"))
+    slab_geometry = jnp.sum(lax.all_gather(picked, ("prow", "pcol"), axis=0), axis=0)
     slab_count = slab_ids.shape[0]
     count = pivots.shape[0] // 2
     tile_width = slab_count // (col_count * col_count)

time: 190 us -> 192 us (1.011)
  blocking collectives: 48.1 us -> 51.9 us
  Pallas kernels: 120 us -> 118 us
    all_gather x0 -> x1, blocking collectives: none -> 45.2 us  [body(): lax.all_gather(picked, ('prow', 'pcol'), axis=0)]
    psum x1 -> x0, blocking collectives: 42.1 us -> none  [body(): slab_geometry = lax.psum(picked, ('prow', 'pcol'))]
where the time goes in v2:
time: 192 us
  Pallas kernels  118 us (61%)
  blocking collectives  51.9 us (27%)
  local copies, waits for them, and re-layouts  12.7 us (7%)
  other arithmetic  5.56 us (3%)
  matrix products  2.64 us (1%)
    pallas_call x1, Pallas kernels, body(): pl.pallas_call(lambda *refs: rows_kernel(own_elim, own_trail, count, *ref...  73.7 us
    all_gather x1, blocking collectives, body(): lax.all_gather(picked, ('prow', 'pcol'), axis=0)  45.2 us
    pallas_call x1, Pallas kernels, body(): pl.pallas_call(lambda *refs: factor_kernel(own_elim, own_trail, *refs), o...  44.5 us
    all_gather x1, blocking collectives, body(): row_geometry = lax.all_gather(panels, 'pcol', axis=1, tiled=True)  6.69 us
    unnamed x1, local copies, waits for them, and re-layouts  3.89 us

profile of v2, /device:TPU:0, one launch (start us, length us, event | category | flops | bytes accessed | tf_op | source)
XLA Modules:
  0.0 191.9 jit_solution(276707450229749335)
XLA Ops:
  0.7 0.9 slice.108
  1.5 0.7 fusion.22
  2.2 0.8 reshape.139
  3.0 0.1 concatenate.47
  3.2 2.6 %fusion.4 = f32[1,7,1024]{2,1,0:T(8,128)S(1)} fusion(f32[7,1024]{1,0:T(8,128)} %param.3, s32[1024]{0:T(1024)S(1)} %iota_add_fusion, s32[1024]{0:T(1024)} %param.4), kind=kOutput, calls=%fused_computation.7 | convolution fusion | flops 89128960 | bytes 65536 | tf_op jit(solution)/shard_map/dot_general | solution.py:296
  5.8 6.7 %all_gather.11 = f32[7,4096]{1,0:T(8,128)S(1)} all-gather(f32[7,1024]{1,0:T(8,128)} %param.3), channel_id=1, replica_groups=mesh['prow'=8,'pcol'=4] {'pcol'}, dimensions={1}, use_global_device_ids=true | all-gather | bytes 143360 | tf_op jit(solution)/shard_map/all_gather | solution.py:289
  12.6 0.1 stack.82.refs_0_
  12.7 45.2 %all-gather.1 = f32[32,7,1024]{2,1,0:T(8,128)S(1)} all-gather(f32[1,7,1024]{2,1,0:T(8,128)S(1)} %fusion.4), channel_id=2, replica_groups=mesh['prow'=8,'pcol'=4] {'prow','pcol'}, dimensions={0}, use_global_device_ids=true | all-gather | bytes 946176 | tf_op jit(solution)/shard_map/all_gather | solution.py:297
  57.9 0.1 reduce_sum.36
  58.1 0.1 reshape.137
  58.2 0.1 dynamic-slice_reduce_fusion
  58.2 0.1 reshape.138
  58.3 0.1 slice.140
  58.5 0.1 stack.71.refs_1_
  58.5 0.1 copy.28
  58.7 0.1 copy.31
  58.8 44.5 %shard_map.58 = (f32[256,448]{1,0:T(8,128)S(1)}, f32[256,448]{1,0:T(8,128)S(1)}, f32[256,64]{1,0:T(8,128)S(1)}, f32[256,64]{1,0:T(8,128)S(1)}, f32[256,256]{1,0:T(8,128)S(1)}, /*index=5*/f32[256,256]{1,0:T(8,128)S(1)}) custom-call(f32[256,8]{1,0:T(8,128)S(1)} %bitcast.63, f32[16,448]{1,0:T(8,128)S(1)} %stack.71.refs_1_, s32[8,64]{1,0:T(8,128)S(1)} %broadcast_in_dim.90.refs_2_), custom_call_target="tpu_custom_call" | custom-call | tf_op jit(solution)/shard_map/pallas_call | solution.py:321
  103.3 0.2 select_reduce_fusion
  103.6 0.1 select_reduce_fusion.2
  103.7 0.1 fusion.11
  103.8 0.1 copy.34.refs_4_
  103.9 0.1 copy.33
  104.1 0.1 copy.32
  104.2 0.1 fusion.7
  104.4 0.3 multiply_subtract_fusion.1
  104.7 0.1 add_select_fusion
  104.8 0.1 slice.147
  104.9 0.1 slice.150
  105.0 0.1 slice.148
  105.2 0.1 slice.143
  105.3 0.1 maximum_bitcast_fusion.3
  105.4 0.1 maximum_bitcast_fusion.5
  105.6 0.1 maximum_bitcast_fusion.2
  105.8 0.4 copy.29
  106.2 0.1 maximum_bitcast_fusion.4
  106.3 1.2 copy.30
  107.5 1.9 stack.79
  109.4 1.8 stack.75
  111.2 3.1 %pad_maximum_fusion = f32[1,4,64,2,512]{2,1,4,3,0:T(4,128)} fusion(f32[1,4,64,1,512]{2,1,4,3,0:T(4,128)S(1)} %stack.79, f32[1,4,64,1,512]{2,1,4,3,0:T(4,128)} %stack.75), kind=kLoop, calls=%fused_computation.2 | loop fusion | flops 262144 | bytes 2097152 | tf_op jit(solution)/shard_map/stack | solution.py:367
  114.3 3.9 %copy.35 = f32[1,4,64,2,512]{4,3,2,1,0:T(2,128)} copy(f32[1,4,64,2,512]{2,1,4,3,0:T(4,128)} %pad_maximum_fusion) | data formatting | bytes 2097152
  118.2 73.7 %shard_map.59 = (f32[64,2,2,4096]{3,2,1,0:T(2,128)}, f32[192,2,2,4096]{3,2,1,0:T(2,128)}) custom-call(f32[8,4096]{1,0:T(8,128)S(1)} %stack.82.refs_0_, f32[448,16]{1,0:T(8,128)S(1)} %bitcast.62, bf16[512,512]{1,0:T(8,128)(2,1)S(1)} %get-tuple-element.45.refs_2_, bf16[512,512]{1,0:T(8,128)(2,1)S(1)} %get-tuple-element.44.refs_3_, f32[64,4]{1,0:T(8,128)S(1)} %copy.34.refs_4_), custom_call_target="tpu_custom_call" | custom-call | tf_op jit(solution)/shard_map/pallas_call | solution.py:388
  (30 shorter events, 0.4 us)
